TPU v7x, 32 devices: a whole 2x2x4 slice. The times are simulated.
32 devices in a mesh: groups: 2 (over x), seq: 16 (over z, y, core).
Axes of the slice: x: 2, y: 2, z: 4, core: 2. Of those that a mesh axis runs over, the one named last changes fastest.
Arguments:
- tokens: bfloat16 [8192, 256], P(('groups', 'seq')), parts along dimension 0, may hold values from -6 to 6
- norm_gain: float32 [256], replicated, may hold values from 0.1 to 1.9
- w_in: bfloat16 [256, 768], replicated, may hold values from -0.375 to 0.375
- short_filter: float32 [3, 768], replicated, may hold values from -0.8 to 0.8
- long_filter: float32 [4096, 256], P('seq'), may hold values from -0.09375 to 0.09375
- medium_filter: float32 [128, 256], replicated, may hold values from -0.5 to 0.5
- skip_gain: float32 [256], replicated, may hold values from -1 to 1
- w_out: bfloat16 [256, 256], replicated, may hold values from -0.375 to 0.375
Outputs:
- result: bfloat16 [8192, 256], P(('groups', 'seq')), parts along dimension 0
There are 2 independent parts, one for each index of `groups`. A program takes and returns all parts, laid end to end along the dimension named above; an argument that names none is the same for every part. Nothing has to cross between parts.
All inputs are finite; a program needn't handle non-finite values.
Results may differ from a plain program's by a relative error of at most 0.015.
Values may be sent and summed in bfloat16 or wider, within the bound.
A program may use at most 64 MiB of HBM per device.

v0:
```python
import math

import jax
import jax.numpy as jnp
from jax import lax
from jax.sharding import PartitionSpec as P

epsilon = 1e-06
highest = lax.Precision.HIGHEST


def from_behind(array, axis, by):
    devices = lax.axis_size(axis)
    pairs = [(i, i + by) for i in range(devices) if 0 <= i + by < devices]
    return lax.ppermute(array, axis, pairs)


def from_partner(array, axis, distance):
    return lax.ppermute(array, axis, [(i, i ^ 1 << distance) for i in range(lax.axis_size(axis))])


def reverse_bits(my_index, bit_count):
    flipped = jnp.zeros((), jnp.int32)
    for bit_num in range(bit_count):
        flipped = flipped + my_index // 2**bit_num % 2 * 2 ** (bit_count - 1 - bit_num)
    return flipped


def phase_table(first, second, modulus):
    products = first[:, None] * second[None, :] % modulus
    phase_angle = 2.0 * math.pi / modulus * products.astype(jnp.float32)
    return (jnp.cos(phase_angle), jnp.sin(phase_angle))


def spectral_middle(current, column, tok_rows, full_len):
    freq_one = 2 * column + jnp.arange(2, dtype=jnp.int32)
    offsets = jnp.arange(tok_rows, dtype=jnp.int32)
    tw_cos, tw_sin = phase_table(freq_one, offsets, full_len)
    tw_cos = tw_cos[:, :, None]
    tw_sin = tw_sin[:, :, None]
    real_part = current[0] * tw_cos + current[1] * tw_sin
    imag_part = current[1] * tw_cos - current[0] * tw_sin
    cos_table, sin_table = phase_table(offsets, offsets, tok_rows)
    spec_re = jnp.einsum("kt,setd->sekd", cos_table, real_part, precision=highest) + jnp.einsum(
        "kt,setd->sekd", sin_table, imag_part, precision=highest
    )
    spec_im = jnp.einsum("kt,setd->sekd", cos_table, imag_part, precision=highest) - jnp.einsum(
        "kt,setd->sekd", sin_table, real_part, precision=highest
    )
    prod_re = spec_re[0] * spec_re[1] - spec_im[0] * spec_im[1]
    prod_im = spec_re[0] * spec_im[1] + spec_im[0] * spec_re[1]
    back_re = jnp.einsum("tk,ekd->etd", cos_table, prod_re, precision=highest) - jnp.einsum(
        "tk,ekd->etd", sin_table, prod_im, precision=highest
    )
    back_im = jnp.einsum("tk,ekd->etd", cos_table, prod_im, precision=highest) + jnp.einsum(
        "tk,ekd->etd", sin_table, prod_re, precision=highest
    )
    return jnp.stack([back_re * tw_cos - back_im * tw_sin, back_re * tw_sin + back_im * tw_cos])


def local(tokens, norm_gain, w_in, short_filter, long_filter, medium_filter, skip_gain, w_out):
    tok_rows, chan_width = tokens.shape
    devices = lax.axis_size("seq")
    my_index = lax.axis_index("seq")
    full_len = 2 * tok_rows * devices
    inputs = tokens.astype(jnp.float32)
    mean_sq = jnp.mean(inputs * inputs, axis=-1, keepdims=True)
    normed = (inputs * lax.rsqrt(mean_sq + epsilon) * norm_gain).astype(jnp.bfloat16)
    projected = jnp.dot(normed, w_in, preferred_element_type=jnp.float32).astype(jnp.bfloat16)
    taps_count = short_filter.shape[0]
    rim_rows = from_behind(projected[tok_rows - (taps_count - 1) :], "seq", 1)
    extended = jnp.concatenate([rim_rows, projected], axis=0)
    short_mix = jnp.zeros((tok_rows, projected.shape[1]), jnp.float32)
    for tap_num in range(taps_count):
        begin = taps_count - 1 - tap_num
        short_mix = short_mix + short_filter[tap_num] * extended[begin : begin + tok_rows]
    query_part = short_mix[:, 0:chan_width]
    key_part = short_mix[:, chan_width : 2 * chan_width]
    value_part = short_mix[:, 2 * chan_width : 3 * chan_width]
    signal = key_part * value_part
    med_len = medium_filter.shape[0]
    med_rows = from_behind(
        signal[tok_rows - (med_len - 1) :].astype(jnp.bfloat16), "seq", 1
    ).astype(jnp.float32)
    med_ext = jnp.concatenate([med_rows, signal], axis=0)

    def add_group(group_num, acc):
        for inner in range(8):
            tap_num = group_num * 8 + inner
            weights = lax.dynamic_slice_in_dim(medium_filter, tap_num, 1, 0)
            window = lax.dynamic_slice_in_dim(med_ext, med_len - 1 - tap_num, tok_rows, 0)
            acc = acc + weights * window
        return acc

    med_out = lax.fori_loop(0, med_len // 8, add_group, jnp.zeros_like(signal))
    sig_pair = jnp.stack([signal, long_filter])
    bit_count = devices.bit_length() - 1
    start_phase = 2.0 * math.pi / (2 * devices) * my_index.astype(jnp.float32)
    real_part = jnp.stack([sig_pair, sig_pair * jnp.cos(start_phase)], axis=1)
    imag_part = jnp.stack([jnp.zeros_like(sig_pair), -sig_pair * jnp.sin(start_phase)], axis=1)
    current = jnp.stack([real_part, imag_part])
    for bit_num in reversed(range(bit_count)):
        half_span = 2**bit_num
        blk_span = 2 * half_span
        partner = from_partner(current.astype(jnp.bfloat16), "seq", bit_num).astype(current.dtype)
        is_upper = my_index // half_span % 2 == 1
        phase_angle = (
            2.0 * math.pi / blk_span * (my_index % blk_span - half_span).astype(jnp.float32)
        )
        summed = current + partner
        differ = partner - current
        w_real = jnp.cos(phase_angle)
        w_imag = -jnp.sin(phase_angle)
        upper_val = jnp.stack(
            [differ[0] * w_real - differ[1] * w_imag, differ[0] * w_imag + differ[1] * w_real]
        )
        current = jnp.where(is_upper, upper_val, summed)
    column = reverse_bits(my_index, bit_count)
    current = spectral_middle(current, column, tok_rows, full_len)
    for bit_num in range(bit_count):
        half_span = 2**bit_num
        blk_span = 2 * half_span
        partner = from_partner(current.astype(jnp.bfloat16), "seq", bit_num).astype(current.dtype)
        is_upper = my_index // half_span % 2 == 1
        inner_pos = my_index % blk_span - jnp.where(is_upper, half_span, 0)
        phase_angle = 2.0 * math.pi / blk_span * inner_pos.astype(jnp.float32)
        w_real = jnp.cos(phase_angle)
        w_imag = jnp.sin(phase_angle)
        factor = jnp.where(is_upper, current, partner)
        base_val = jnp.where(is_upper, partner, current)
        scaled = jnp.stack(
            [factor[0] * w_real - factor[1] * w_imag, factor[0] * w_imag + factor[1] * w_real]
        )
        current = jnp.where(is_upper, base_val - scaled, base_val + scaled)
    conv_out = (
        current[0, 0] + current[0, 1] * jnp.cos(start_phase) - current[1, 1] * jnp.sin(start_phase)
    ) / full_len
    mixed_out = (query_part * (conv_out + med_out + skip_gain * signal)).astype(jnp.bfloat16)
    return jnp.dot(mixed_out, w_out, preferred_element_type=jnp.float32).astype(jnp.bfloat16)


def solution(mesh):
    placed = (P(("groups", "seq"), None), P(), P(), P(), P("seq", None), P(), P(), P())
    return jax.shard_map(
        local, mesh=mesh, in_specs=placed, out_specs=P(("groups", "seq"), None), check_vma=False
    )
```

profile of v0, /device:TPU:0, one launch (start us, length us, event | category | flops | bytes accessed | tf_op | source)
XLA Modules:
  0.0 211.3 jit_solution(2216791617882985086)
XLA Ops:
  1.1 1.2 convolution_convert_fusion
  2.4 2.4 %collective-permute-start = (bf16[2,768]{1,0:T(2,128)(2,1)S(1)}, bf16[2,768]{1,0:T(2,128)(2,1)S(1)}, u32[]{:S(2)}, u32[]{:S(2)}) collective-permute-start(bf16[2,768]{1,0:T(2,128)(2,1)S(1)} %slice.163), channel_id=1, source_target_pairs={{0,1},{1,2},{2,3},{3,4},{4,5},{5,6},{6,7},{7,8},{8,9},{9,10},{10,1... | collective-permute-start | bytes 9224 | tf_op jit(solution)/shard_map/ppermute | solution.py:15
  7.1 1.3 fusion.13
  8.3 6.5 %collective-permute-start.1 = (bf16[2,2,2,256,256]{4,3,2,1,0:T(8,128)(2,1)}, bf16[2,2,2,256,256]{4,3,2,1,0:T(8,128)(2,1)S(1)}, u32[]{:S(2)}, u32[]{:S(2)}) collective-permute-start(bf16[2,2,2,256,256]{4,3,2,1,0:T(8,128)(2,1)} %fusion.13), channel_id=1, source_target_pairs={{0,8},{1,9},{2,10},{3,11},{4,12},{5,13},{6,14},{7,15},{8,0},{9,1},... | collective-permute-start | bytes 3145736 | tf_op jit(solution)/shard_map/ppermute | solution.py:19
  15.0 44.6 %collective-permute-done.1 = bf16[2,2,2,256,256]{4,3,2,1,0:T(8,128)(2,1)S(1)} collective-permute-done((bf16[2,2,2,256,256]{4,3,2,1,0:T(8,128)(2,1)}, bf16[2,2,2,256,256]{4,3,2,1,0:T(8,128)(2,1)S(1)}, u32[]{:S(2)}, u32[]{:S(2)}) %collective-permute-start.1) | collective-permute-done | bytes 1048608 | tf_op jit(solution)/shard_map/ppermute | solution.py:19
  60.6 2.9 %fusion.109 = (bf16[2,2,2,256,256]{4,3,2,1,0:T(8,128)(2,1)}, f32[2,2,2,256,256]{4,3,2,1,0:T(8,128)S(1)}) fusion(bf16[2,2,2,256,256]{4,3,2,1,0:T(8,128)(2,1)} %copy-done.6, f32[1,2,2,256,256]{4,3,2,1,0:T(8,128)} %copy-done.3, f32[1,2,2,256,256]{4,3,2,1,0:T(8,128)S(1)} %get-tuple-element.227, f32[1,2,2,256,256]{4,3,2,1,0:T(8,128)S(1)} %get-tuple-element.212, ...), kind=kLoop, calls=%fused_computation.189 | loop fusion | flops 3145728 | bytes 8388609 | tf_op jit(solution)/shard_map/convert_element_type | solution.py:105
  64.5 23.4 %collective-permute-done.2 = bf16[2,2,2,256,256]{4,3,2,1,0:T(8,128)(2,1)S(1)} collective-permute-done((bf16[2,2,2,256,256]{4,3,2,1,0:T(8,128)(2,1)}, bf16[2,2,2,256,256]{4,3,2,1,0:T(8,128)(2,1)S(1)}, u32[]{:S(2)}, u32[]{:S(2)}) %collective-permute-start.2) | collective-permute-done | bytes 1048608 | tf_op jit(solution)/shard_map/ppermute | solution.py:19
  89.1 3.2 %fusion.107 = (bf16[2,2,2,256,256]{4,3,2,1,0:T(8,128)(2,1)}, f32[2,2,2,256,256]{4,3,2,1,0:T(8,128)S(1)}) fusion(f32[2,2,2,256,256]{4,3,2,1,0:T(8,128)} %copy-done.1, bf16[2,2,2,256,256]{4,3,2,1,0:T(8,128)(2,1)} %copy-done.7, f32[1,2,2,256,256]{4,3,2,1,0:T(8,128)S(1)} %get-tuple-element.210, f32[1,2,2,256,256]{4,3,2,1,0:T(8,128)S(1)} %get-tuple-element.209, ...), kind=kLoop, calls=%fused_computation.188 | loop fusion | flops 2621440 | bytes 8388609 | tf_op jit(solution)/shard_map/convert_element_type | solution.py:105
  92.3 1.4 collective-permute-start.3
  94.0 22.2 %collective-permute-done.3 = bf16[2,2,2,256,256]{4,3,2,1,0:T(8,128)(2,1)S(1)} collective-permute-done((bf16[2,2,2,256,256]{4,3,2,1,0:T(8,128)(2,1)}, bf16[2,2,2,256,256]{4,3,2,1,0:T(8,128)(2,1)S(1)}, u32[]{:S(2)}, u32[]{:S(2)}) %collective-permute-start.3) | collective-permute-done | bytes 1048608 | tf_op jit(solution)/shard_map/ppermute | solution.py:19
  116.6 2.1 fusion.105
  119.0 2.5 %collective-permute-done.4 = bf16[2,2,2,256,256]{4,3,2,1,0:T(8,128)(2,1)S(1)} collective-permute-done((bf16[2,2,2,256,256]{4,3,2,1,0:T(8,128)(2,1)}, bf16[2,2,2,256,256]{4,3,2,1,0:T(8,128)(2,1)S(1)}, u32[]{:S(2)}, u32[]{:S(2)}) %collective-permute-start.4) | collective-permute-done | bytes 1048608 | tf_op jit(solution)/shard_map/ppermute | solution.py:19
  121.6 1.8 convert_subtract_fusion
  123.7 1.3 copy-done.2
  125.5 2.8 %fusion.45 = f32[2,2,256,256]{3,2,1,0:T(8,128)S(1)} fusion(f32[2,2,2,256,256]{4,3,2,1,0:T(8,128)S(1)} %fusion.10, f32[2,256]{1,0:T(2,128)S(1)} %get-tuple-element.226, f32[2,256]{1,0:T(2,128)S(1)} %get-tuple-element.225), kind=kOutput, calls=%fused_computation.128 | convolution fusion | flops 807010304 | bytes 3149824 | tf_op jit(solution)/shard_map/kt,setd->sekd/dot_general | solution.py:44
  128.3 2.8 %fusion.43 = f32[2,2,256,256]{3,2,1,0:T(8,128)S(1)} fusion(f32[2,2,2,256,256]{4,3,2,1,0:T(8,128)S(1)} %fusion.10, f32[2,256]{1,0:T(2,128)S(1)} %get-tuple-element.226, f32[2,256]{1,0:T(2,128)S(1)} %get-tuple-element.225), kind=kOutput, calls=%fused_computation.126 | convolution fusion | flops 807010304 | bytes 3149824 | tf_op jit(solution)/shard_map/kt,setd->sekd/dot_general | solution.py:47
  131.1 3.0 %fusion.12 = f32[2,2,256,256]{2,3,1,0:T(8,128)S(1)} fusion(f32[2,2,256,256]{3,2,1,0:T(8,128)S(1)} %fusion.45, f32[2,2,2,256,256]{4,3,2,1,0:T(8,128)S(1)} %fusion.10, f32[2,256]{1,0:T(2,128)S(1)} %get-tuple-element.226, f32[2,256]{1,0:T(2,128)S(1)} %get-tuple-element.225), kind=kOutput, calls=%fused_computation.32 | convolution fusion | flops 807272448 | bytes 4198400 | tf_op jit(solution)/shard_map/kt,setd->sekd/dot_general | solution.py:44
  134.1 2.8 %fusion.11 = f32[2,2,256,256]{2,3,1,0:T(8,128)S(1)} fusion(f32[2,2,256,256]{3,2,1,0:T(8,128)S(1)} %fusion.43, f32[2,2,2,256,256]{4,3,2,1,0:T(8,128)S(1)} %fusion.10, f32[2,256]{1,0:T(2,128)S(1)} %get-tuple-element.226, f32[2,256]{1,0:T(2,128)S(1)} %get-tuple-element.225), kind=kOutput, calls=%fused_computation.30 | convolution fusion | flops 807272448 | bytes 4198400 | tf_op jit(solution)/shard_map/kt,setd->sekd/dot_general | solution.py:47
  137.0 1.6 fusion.15
  138.6 1.6 fusion.19
  140.2 1.6 convolution_add_fusion.1
  141.8 1.7 subtract_bitcast_fusion
  144.0 1.6 collective-permute-done.5
  148.0 13.1 %collective-permute-done.6 = bf16[2,2,256,256]{3,2,1,0:T(8,128)(2,1)S(1)} collective-permute-done((bf16[2,2,256,256]{3,2,1,0:T(8,128)(2,1)}, bf16[2,2,256,256]{3,2,1,0:T(8,128)(2,1)S(1)}, u32[]{:S(2)}, u32[]{:S(2)}) %collective-permute-start.6) | collective-permute-done | bytes 524320 | tf_op jit(solution)/shard_map/ppermute | solution.py:19
  162.3 2.4 %collective-permute-start.7 = (bf16[2,2,256,256]{3,2,1,0:T(8,128)(2,1)}, bf16[2,2,256,256]{3,2,1,0:T(8,128)(2,1)S(1)}, u32[]{:S(2)}, u32[]{:S(2)}) collective-permute-start(bf16[2,2,256,256]{3,2,1,0:T(8,128)(2,1)} %get-tuple-element.185), channel_id=1, source_target_pairs={{0,4},{1,5},{2,6},{3,7},{4,0},{5,1},{6,2},{7,3},{8,12},{9,13},{10,... | collective-permute-start | bytes 1572872 | tf_op jit(solution)/shard_map/ppermute | solution.py:19
  164.8 1.3 collective-permute-start.9
  167.0 9.3 %collective-permute-done.7 = bf16[2,2,256,256]{3,2,1,0:T(8,128)(2,1)S(1)} collective-permute-done((bf16[2,2,256,256]{3,2,1,0:T(8,128)(2,1)}, bf16[2,2,256,256]{3,2,1,0:T(8,128)(2,1)S(1)}, u32[]{:S(2)}, u32[]{:S(2)}) %collective-permute-start.7) | collective-permute-done | bytes 524320 | tf_op jit(solution)/shard_map/ppermute | solution.py:19
  177.1 2.1 fusion.102
  179.2 3.6 %collective-permute-start.8 = (bf16[2,2,256,256]{3,2,1,0:T(8,128)(2,1)}, bf16[2,2,256,256]{3,2,1,0:T(8,128)(2,1)S(1)}, u32[]{:S(2)}, u32[]{:S(2)}) collective-permute-start(bf16[2,2,256,256]{3,2,1,0:T(8,128)(2,1)} %get-tuple-element.183), channel_id=1, source_target_pairs={{0,8},{1,9},{2,10},{3,11},{4,12},{5,13},{6,14},{7,15},{8,0},{9,1},... | collective-permute-start | bytes 1572872 | tf_op jit(solution)/shard_map/ppermute | solution.py:19
  182.8 23.6 %while.17 = (s32[]{:T(128)}, f32[256,256]{1,0:T(8,128)S(1)}, f32[128,256]{1,0:T(8,128)}, f32[383,256]{1,0:T(8,128)S(1)}, s32[]{:T(128)}, /*index=5*/s32[]{:T(128...) while((s32[]{:T(128)}, f32[256,256]{1,0:T(8,128)S(1)}, ...), condition=%wide.region_2.0_spmd.clone, body=%wide.region_1.0_spmd.clone.sunk | while | flops 1114179 | bytes 2647031 | solution.py:95
  207.2 1.2 convert_select_fusion
  209.4 1.8 convolution_convert_fusion.1
  (103 shorter events, 35.8 us)
Async XLA Ops:
  0.0 1.1 copy-start
  0.0 6.1 %copy-start.11 = (f32[256,256]{1,0:T(8,128)S(1)}, f32[256,256]{1,0:T(8,128)}, u32[]{:S(2)}) copy-start(f32[256,256]{1,0:T(8,128)} %param.14) | copy-start | bytes 786436
  2.4 3.4 %collective-permute-start = (bf16[2,768]{1,0:T(2,128)(2,1)S(1)}, bf16[2,768]{1,0:T(2,128)(2,1)S(1)}, u32[]{:S(2)}, u32[]{:S(2)}) collective-permute-start(bf16[2,768]{1,0:T(2,128)(2,1)S(1)} %slice.163), channel_id=1, source_target_pairs={{0,1},{1,2},{2,3},{3,4},{4,5},{5,6},{6,7},{7,8},{8,9},{9,10},{10,1... | collective-permute-start | bytes 9224 | tf_op jit(solution)/shard_map/ppermute | solution.py:15
  6.0 0.9 copy-start.4
  7.1 52.8 %copy-start.3 = (f32[1,2,2,256,256]{4,3,2,1,0:T(8,128)}, f32[1,2,2,256,256]{4,3,2,1,0:T(8,128)S(1)}, u32[]{:S(2)}) copy-start(f32[1,2,2,256,256]{4,3,2,1,0:T(8,128)S(1)} %get-tuple-element.228) | copy-start | bytes 3145732
  8.3 51.3 %collective-permute-start.1 = (bf16[2,2,2,256,256]{4,3,2,1,0:T(8,128)(2,1)}, bf16[2,2,2,256,256]{4,3,2,1,0:T(8,128)(2,1)S(1)}, u32[]{:S(2)}, u32[]{:S(2)}) collective-permute-start(bf16[2,2,2,256,256]{4,3,2,1,0:T(8,128)(2,1)} %fusion.13), channel_id=1, source_target_pairs={{0,8},{1,9},{2,10},{3,11},{4,12},{5,13},{6,14},{7,15},{8,0},{9,1},... | collective-permute-start | bytes 3145736 | tf_op jit(solution)/shard_map/ppermute | solution.py:19
  59.6 1.0 copy-start.6
  63.5 24.6 %copy-start.1 = (f32[2,2,2,256,256]{4,3,2,1,0:T(8,128)}, f32[2,2,2,256,256]{4,3,2,1,0:T(8,128)S(1)}, u32[]{:S(2)}) copy-start(f32[2,2,2,256,256]{4,3,2,1,0:T(8,128)S(1)} %get-tuple-element.194) | copy-start | bytes 6291460
  63.6 24.3 %collective-permute-start.2 = (bf16[2,2,2,256,256]{4,3,2,1,0:T(8,128)(2,1)}, bf16[2,2,2,256,256]{4,3,2,1,0:T(8,128)(2,1)S(1)}, u32[]{:S(2)}, u32[]{:S(2)}) collective-permute-start(bf16[2,2,2,256,256]{4,3,2,1,0:T(8,128)(2,1)} %get-tuple-element.193), channel_id=1, source_target_pairs={{0,4},{1,5},{2,6},{3,7},{4,0},{5,1},{6,2},{7,3},{8,12},{9,13},{10,... | collective-permute-start | bytes 3145736 | tf_op jit(solution)/shard_map/ppermute | solution.py:19
  87.9 1.0 copy-start.7
  92.3 23.8 %collective-permute-start.3 = (bf16[2,2,2,256,256]{4,3,2,1,0:T(8,128)(2,1)}, bf16[2,2,2,256,256]{4,3,2,1,0:T(8,128)(2,1)S(1)}, u32[]{:S(2)}, u32[]{:S(2)}) collective-permute-start(bf16[2,2,2,256,256]{4,3,2,1,0:T(8,128)(2,1)} %get-tuple-element.191), channel_id=1, source_target_pairs={{0,2},{1,3},{2,0},{3,1},{4,6},{5,7},{6,4},{7,5},{8,10},{9,11},{10,... | collective-permute-start | bytes 3145736 | tf_op jit(solution)/shard_map/ppermute | solution.py:19
  118.7 2.9 %collective-permute-start.4 = (bf16[2,2,2,256,256]{4,3,2,1,0:T(8,128)(2,1)}, bf16[2,2,2,256,256]{4,3,2,1,0:T(8,128)(2,1)S(1)}, u32[]{:S(2)}, u32[]{:S(2)}) collective-permute-start(bf16[2,2,2,256,256]{4,3,2,1,0:T(8,128)(2,1)} %get-tuple-element.189), channel_id=1, source_target_pairs={{0,1},{1,0},{2,3},{3,2},{4,5},{5,4},{6,7},{7,6},{8,9},{9,8},{10,11... | collective-permute-start | bytes 3145736 | tf_op jit(solution)/shard_map/ppermute | solution.py:19
  123.5 1.6 copy-start.2
  143.6 2.0 collective-permute-start.5
  146.9 14.2 %collective-permute-start.6 = (bf16[2,2,256,256]{3,2,1,0:T(8,128)(2,1)}, bf16[2,2,256,256]{3,2,1,0:T(8,128)(2,1)S(1)}, u32[]{:S(2)}, u32[]{:S(2)}) collective-permute-start(bf16[2,2,256,256]{3,2,1,0:T(8,128)(2,1)} %get-tuple-element.187), channel_id=1, source_target_pairs={{0,2},{1,3},{2,0},{3,1},{4,6},{5,7},{6,4},{7,5},{8,10},{9,11},{10,... | collective-permute-start | bytes 1572872 | tf_op jit(solution)/shard_map/ppermute | solution.py:19
  161.3 3.4 %copy-start.5 = (f32[256,768]{1,0:T(8,128)S(1)}, f32[256,768]{1,0:T(8,128)}, u32[]{:S(2)}) copy-start(f32[256,768]{1,0:T(8,128)} %copy-done.4) | copy-start | bytes 2359300
  162.3 14.0 %collective-permute-start.7 = (bf16[2,2,256,256]{3,2,1,0:T(8,128)(2,1)}, bf16[2,2,256,256]{3,2,1,0:T(8,128)(2,1)S(1)}, u32[]{:S(2)}, u32[]{:S(2)}) collective-permute-start(bf16[2,2,256,256]{3,2,1,0:T(8,128)(2,1)} %get-tuple-element.185), channel_id=1, source_target_pairs={{0,4},{1,5},{2,6},{3,7},{4,0},{5,1},{6,2},{7,3},{8,12},{9,13},{10,... | collective-permute-start | bytes 1572872 | tf_op jit(solution)/shard_map/ppermute | solution.py:19
  164.8 2.2 %collective-permute-start.9 = (bf16[127,256]{1,0:T(8,128)(2,1)S(1)}, bf16[127,256]{1,0:T(8,128)(2,1)S(1)}, u32[]{:S(2)}, u32[]{:S(2)}) collective-permute-start(bf16[127,256]{1,0:T(8,128)(2,1)S(1)} %slice.293), channel_id=1, source_target_pairs={{0,1},{1,2},{2,3},{3,4},{4,5},{5,6},{6,7},{7,8},{8,9},{9,10},{10,1... | collective-permute-start | bytes 195080 | tf_op jit(solution)/shard_map/ppermute | solution.py:15
  176.3 0.8 copy-start.8
  179.2 27.2 %collective-permute-start.8 = (bf16[2,2,256,256]{3,2,1,0:T(8,128)(2,1)}, bf16[2,2,256,256]{3,2,1,0:T(8,128)(2,1)S(1)}, u32[]{:S(2)}, u32[]{:S(2)}) collective-permute-start(bf16[2,2,256,256]{3,2,1,0:T(8,128)(2,1)} %get-tuple-element.183), channel_id=1, source_target_pairs={{0,8},{1,9},{2,10},{3,11},{4,12},{5,13},{6,14},{7,15},{8,0},{9,1},... | collective-permute-start | bytes 1572872 | tf_op jit(solution)/shard_map/ppermute | solution.py:19
  206.4 0.8 copy-start.9
  207.2 1.4 copy-start.10
  208.5 0.9 copy-start.12
  208.5 0.9 copy-start.13
where the time goes:
time: 213 us; the launch traced here: 211 us
  waiting for transfers between devices  117 us (55%)
  other arithmetic  26.9 us (13%)
  local copies, waits for them, and re-layouts  22.4 us (11%)
  matrix products  21 us (10%)
  starting transfers between devices  19.4 us (9%)
  loops' own time  2.25 us (1%)
    ppermute x8, waiting for transfers between devices, from_partner(): lax.ppermute(array, axis, [(i, i ^ 1 << distance) for i in range(lax.axis...  117 us
    dynamic_slice x16, local copies, waits for them, and re-layouts, add_group(): weights = lax.dynamic_slice_in_dim(medium_filter, tap_num, 1, 0)  16.2 us
    ppermute x8, starting transfers between devices, from_partner(): lax.ppermute(array, axis, [(i, i ^ 1 << distance) for i in range(lax.axis...  15.8 us
    convert_element_type x8, other arithmetic, local(): current.astype(jnp.bfloat16)  13.7 us
    unnamed x28, local copies, waits for them, and re-layouts  5.32 us
    add x16, other arithmetic, add_group(): acc = acc + weights * window  5.1 us
  transfers between devices with their start and end apart: 10, of which 8 were waited for; matrix products, arithmetic and copies ran while one was open for 11% of the time, Pallas kernels for 0%

commit v1 on v0

v1 whole, which is shorter than its diff:
```python
import math

import jax
import jax.numpy as jnp
import numpy as np
from jax import lax
from jax.sharding import PartitionSpec as P

epsilon = 1e-06
bf16 = jnp.bfloat16
f32 = jnp.float32


def tables(devices, tok_rows, chans):
    full = devices * tok_rows
    idx = np.arange(devices)
    angle = 2.0 * math.pi * ((idx[:, None] * (4 * idx[None, :] + 1)) % (4 * devices)) / (4 * devices)
    eye = np.eye(chans)
    outer_cos = np.kron(np.cos(angle), eye)
    outer_sin = np.kron(np.sin(angle), eye)
    first = np.concatenate([outer_cos.T, -outer_sin.T], axis=0)
    last = np.concatenate([outer_cos, -outer_sin], axis=1) / full
    pos = np.arange(tok_rows)
    turn = 2.0 * math.pi * ((4 * idx[:, None] + 1) * pos[None, :]) / (4 * full)
    tw_cos = np.repeat(np.cos(turn), chans, axis=0)
    tw_sin = np.repeat(np.sin(turn), chans, axis=0)
    inner = 2.0 * math.pi * (pos[:, None] * pos[None, :] % tok_rows) / tok_rows
    cos_t, sin_t = np.cos(inner), np.sin(inner)
    middle = np.block([[cos_t, -sin_t], [sin_t, cos_t]])
    return (
        first.astype(bf16),
        middle.astype(bf16),
        last.astype(bf16),
        tw_cos.astype(np.float32),
        tw_sin.astype(np.float32),
    )


def dot(a, b):
    return jnp.dot(a, b, preferred_element_type=f32)


def forward(rows, first, middle, tw_cos, tw_sin):
    half = rows.shape[0]
    part = dot(first, rows)
    re, im = part[:half], part[half:]
    turned = jnp.concatenate([re * tw_cos + im * tw_sin, im * tw_cos - re * tw_sin], axis=1)
    return dot(turned.astype(bf16), middle)


def convolve(sig, fil, first, middle, last, tw_cos, tw_sin):
    width = sig.shape[1]
    spec = forward(sig, first, middle, tw_cos, tw_sin)
    gain = forward(fil, first, middle, tw_cos, tw_sin)
    sr, si, gr, gi = spec[:, :width], spec[:, width:], gain[:, :width], gain[:, width:]
    prod = jnp.concatenate([sr * gi + si * gr, sr * gr - si * gi], axis=1).astype(bf16)
    back = dot(prod, middle)
    im, re = back[:, :width], back[:, width:]
    turned = jnp.concatenate([re * tw_cos - im * tw_sin, re * tw_sin + im * tw_cos], axis=0)
    return dot(last, turned.astype(bf16))


def from_behind(array, axis, by):
    devices = lax.axis_size(axis)
    pairs = [(i, i + by) for i in range(devices) if 0 <= i + by < devices]
    return lax.ppermute(array, axis, pairs)


def local(tokens, norm_gain, w_in, short_filter, long_filter, medium_filter, skip_gain, w_out):
    tok_rows, chan_width = tokens.shape
    devices = lax.axis_size("seq")
    my_index = lax.axis_index("seq")
    chans = chan_width // devices
    consts = [jnp.asarray(t) for t in tables(devices, tok_rows, chans)]
    med = jnp.pad(medium_filter, ((0, tok_rows - medium_filter.shape[0]), (0, 0)))
    med = med.at[0].add(skip_gain)
    taps = (long_filter + jnp.where(my_index == 0, med, 0.0)).astype(bf16)
    inputs = tokens.astype(f32)
    mean_sq = jnp.mean(inputs * inputs, axis=-1, keepdims=True)
    normed = (inputs * lax.rsqrt(mean_sq + epsilon) * norm_gain).astype(bf16)
    projected = dot(normed, w_in).astype(bf16)
    taps_count = short_filter.shape[0]
    rim_rows = from_behind(projected[tok_rows - (taps_count - 1) :], "seq", 1)
    extended = jnp.concatenate([rim_rows, projected], axis=0)
    short_mix = jnp.zeros((tok_rows, projected.shape[1]), f32)
    for tap_num in range(taps_count):
        begin = taps_count - 1 - tap_num
        short_mix = short_mix + short_filter[tap_num] * extended[begin : begin + tok_rows]
    query_part = short_mix[:, 0:chan_width]
    signal = short_mix[:, chan_width : 2 * chan_width] * short_mix[:, 2 * chan_width :]

    def spread(array):
        split = array.astype(bf16).T.reshape(devices, chans, tok_rows)
        return lax.all_to_all(split, "seq", 0, 0, tiled=True).reshape(chan_width, tok_rows)

    mixed = convolve(spread(signal), spread(taps), *consts)
    back = spread_back(mixed, devices, chans)
    mixed_out = (query_part * back.T.astype(f32)).astype(bf16)
    return dot(mixed_out, w_out).astype(bf16)


def spread_back(mixed, devices, chans):
    split = mixed.astype(bf16).reshape(devices, chans, mixed.shape[1])
    return lax.all_to_all(split, "seq", 0, 0, tiled=True).reshape(mixed.shape)


def solution(mesh):
    placed = (P(("groups", "seq"), None), P(), P(), P(), P("seq", None), P(), P(), P())
    return jax.shard_map(
        local, mesh=mesh, in_specs=placed, out_specs=P(("groups", "seq"), None), check_vma=False
    )
```

time: 213 us -> 48.4 us (0.23)
  waiting for transfers between devices: 117 us -> 8.96 us
  other arithmetic: 26.9 us -> 1.83 us
  matrix products: 21 us -> 3.49 us
  local copies, waits for them, and re-layouts: 22.4 us -> 7.76 us
  blocking collectives: 0 us -> 10.5 us
  starting transfers between devices: 19.4 us -> 15 us
  loops' own time: 2.25 us -> 0 us
    ppermute x8 -> x0, waiting for transfers between devices: 117 us -> none  [from_partner(): lax.ppermute(array, axis, [(i, i ^ 1 << distance) for i in range(lax.axis...]
    dot_general x10 -> x12, matrix products: 21 us -> 3.49 us  [dot(): return jnp.dot(a, b, preferred_element_type=f32)]
    dynamic_slice x16 -> x0, local copies, waits for them, and re-layouts: 16.2 us -> none  [add_group(): weights = lax.dynamic_slice_in_dim(medium_filter, tap_num, 1, 0)]
    ppermute x8 -> x0, starting transfers between devices: 15.8 us -> none  [from_partner(): lax.ppermute(array, axis, [(i, i ^ 1 << distance) for i in range(lax.axis...]
    convert_element_type x9 -> x2, other arithmetic: 13.7 us -> 0.72 us  [the longest x1 0.69 us: local(): taps = (long_filter + jnp.where(my_index == 0, med, 0.0)).astype(bf16)]
    all_to_all x0 -> x2, starting transfers between devices: none -> 12.7 us  [spread(): lax.all_to_all(split, 'seq', 0, 0, tiled=True).reshape(chan_width, tok_rows)]
    all_to_all x0 -> x1, blocking collectives: none -> 10.5 us  [spread_back(): return lax.all_to_all(split, 'seq', 0, 0, tiled=True).reshape(mixed.shape)]
    all_to_all x0 -> x2, waiting for transfers between devices: none -> 8.2 us  [spread(): lax.all_to_all(split, 'seq', 0, 0, tiled=True).reshape(chan_width, tok_rows)]
  transfers between devices with their start and end apart: 10 -> 3, of which waited for: 8 -> 3; matrix products, arithmetic and copies ran while one was open for 11% -> 5% of each run, Pallas kernels for 0% -> 0%
where the time goes in v1:
time: 48.4 us; the launch traced here: 47.9 us
  starting transfers between devices  15 us (31%)
  blocking collectives  10.5 us (22%)
  waiting for transfers between devices  8.96 us (19%)
  local copies, waits for them, and re-layouts  7.76 us (16%)
  matrix products  3.49 us (7%)
  other arithmetic  1.83 us (4%)
    all_to_all x2, starting transfers between devices, spread(): lax.all_to_all(split, 'seq', 0, 0, tiled=True).reshape(chan_width, tok_rows)  12.7 us
    all_to_all x1, blocking collectives, spread_back(): return lax.all_to_all(split, 'seq', 0, 0, tiled=True).reshape(mixed.shape)  10.5 us
    all_to_all x2, waiting for transfers between devices, spread(): lax.all_to_all(split, 'seq', 0, 0, tiled=True).reshape(chan_width, tok_rows)  8.2 us
    unnamed x30, local copies, waits for them, and re-layouts  6.2 us
    dot_general x12, matrix products, dot(): return jnp.dot(a, b, preferred_element_type=f32)  3.49 us
    ppermute x1, starting transfers between devices, from_behind(): return lax.ppermute(array, axis, pairs)  2.31 us
  transfers between devices with their start and end apart: 3, of which 3 were waited for; matrix products, arithmetic and copies ran while one was open for 5% of the time, Pallas kernels for 0%

profile of v1, /device:TPU:0, one launch (start us, length us, event | category | flops | bytes accessed | tf_op | source)
XLA Modules:
  0.0 47.9 jit_solution(16273044202253010826)
XLA Ops:
  0.0 1.1 %copy.21 = f32[128,256]{0,1:T(8,128)S(1)} copy(f32[128,256]{1,0:T(8,128)} %param.20) | data formatting | bytes 262144 | tf_op args[5]
  1.1 0.7 %copy-done.13 = f32[256]{0:T(256)S(1)} copy-done((f32[256]{0:T(256)S(1)}, f32[256]{0:T(256)}, u32[]{:S(2)}) %copy-start.13) | copy-done | bytes 1048
  1.8 0.7 %slice_add_fusion = f32[1,256]{1,0:T(1,128)S(1)} fusion(f32[1,256]{1,0:T(1,128)S(1)} %bitcast.35, f32[128,256]{1,0:T(8,128)} %param.20), kind=kLoop, calls=%fused_computation.41 | loop fusion | flops 256 | bytes 3072 | tf_op jit(solution)/shard_map/add | solution.py:76
  2.8 0.5 %scatter-add.4 = f32[256,256]{0,1:T(8,128)S(1)} dynamic-update-slice(f32[256,256]{0,1:T(8,128)S(1)} %pad.6, f32[1,256]{0,1:T(8,128)S(1)} %copy.22, s32[]{:T(128)} %constant.50.clone.1, s32[]{:T(128)} %constant.50.clone.1) | dynamic-update-slice | bytes 2052 | tf_op jit(solution)/shard_map/scatter-add | solution.py:76
  3.3 0.7 %add_convert_fusion.3 = bf16[256,256]{0,1:T(8,128)(2,1)} fusion(f32[256,256]{0,1:T(8,128)S(1)} %copy.23, f32[256,256]{0,1:T(8,128)S(1)} %scatter-add.4, pred[]{:T(512)S(6)} %eq.3), kind=kLoop, calls=%fused_computation.27 | loop fusion | flops 196608 | bytes 655361 | tf_op jit(solution)/shard_map/convert_element_type | solution.py:77
  4.0 7.5 %all-to-all-start.1 = ((bf16[16,16,256]{2,1,0:T(8,128)(2,1)}), bf16[16,16,256]{2,1,0:T(8,128)(2,1)S(1)}, u32[]{:S(2)}, u32[]{:S(2)}) async-start(bf16[16,16,256]{2,1,0:T(8,128)(2,1)} %bitcast.5), calls=%async_computation.1 | async-start | bytes 262144 | tf_op jit(solution)/shard_map/all_to_all | solution.py:94
  11.6 0.6 %copy-done.12 = f32[256]{0:T(256)S(1)} copy-done((f32[256]{0:T(256)S(1)}, f32[256]{0:T(256)}, u32[]{:S(2)}) %copy-start.12) | copy-done | bytes 1048
  12.3 0.3 convolution_convert_fusion
  12.6 2.3 %collective-permute-start = (bf16[2,768]{1,0:T(2,128)(2,1)S(1)}, bf16[2,768]{1,0:T(2,128)(2,1)S(1)}, u32[]{:S(2)}, u32[]{:S(2)}) collective-permute-start(bf16[2,768]{1,0:T(2,128)(2,1)S(1)} %slice.103), channel_id=1, source_target_pairs={{0,1},{1,2},{2,3},{3,4},{4,5},{5,6},{6,7},{7,8},{8,9},{9,10},{10,1... | collective-permute-start | bytes 9224 | tf_op jit(solution)/shard_map/ppermute | solution.py:66
  15.0 0.8 %collective-permute-done = bf16[2,768]{1,0:T(2,128)(2,1)S(1)} collective-permute-done((bf16[2,768]{1,0:T(2,128)(2,1)S(1)}, bf16[2,768]{1,0:T(2,128)(2,1)S(1)}, u32[]{:S(2)}, u32[]{:S(2)}) %collective-permute-start) | collective-permute-done | bytes 3104 | tf_op jit(solution)/shard_map/ppermute | solution.py:66
  15.7 0.3 multiply_add_fusion
  16.1 0.8 %copy.20 = bf16[256,256]{1,0:T(8,128)(2,1)} copy(bf16[256,256]{0,1:T(8,128)(2,1)S(1)} %fusion.12) | data formatting | bytes 262144 | tf_op jit(solution)/shard_map/transpose | solution.py:93
  16.8 2.6 %all-to-all-done.1 = bf16[16,16,256]{2,1,0:T(8,128)(2,1)S(1)} async-done(((bf16[16,16,256]{2,1,0:T(8,128)(2,1)}), bf16[16,16,256]{2,1,0:T(8,128)(2,1)S(1)}, u32[]{:S(2)}, u32[]{:S(2)}) %all-to-all-start.1) | async-done | bytes 131104 | tf_op jit(solution)/shard_map/all_to_all | solution.py:94
  19.4 5.2 %all-to-all-start = ((bf16[16,16,256]{2,1,0:T(8,128)(2,1)}), bf16[16,16,256]{2,1,0:T(8,128)(2,1)S(1)}, u32[]{:S(2)}, u32[]{:S(2)}) async-start(bf16[16,16,256]{2,1,0:T(8,128)(2,1)} %bitcast.1), calls=%async_computation | async-start | bytes 262144 | tf_op jit(solution)/shard_map/all_to_all | solution.py:94
  24.7 0.2 fusion.17
  24.9 0.7 %copy-done.1 = f32[256,256]{1,0:T(8,128)S(1)} copy-done((f32[256,256]{1,0:T(8,128)S(1)}, f32[256,256]{1,0:T(8,128)}, u32[]{:S(2)}) %copy-start.1) | copy-done | bytes 262168
  25.8 0.2 fusion.8
  26.0 0.7 %copy-done.4 = bf16[256,512]{1,0:T(8,128)(2,1)S(1)} copy-done((bf16[256,512]{1,0:T(8,128)(2,1)S(1)}, bf16[256,512]{1,0:T(8,128)(2,1)}, u32[]{:S(2)}) %copy-start.4) | copy-done | bytes 262168
  26.7 0.2 convolution_add_fusion.1
  27.0 5.6 %all-to-all-done = bf16[16,16,256]{2,1,0:T(8,128)(2,1)S(1)} async-done(((bf16[16,16,256]{2,1,0:T(8,128)(2,1)}), bf16[16,16,256]{2,1,0:T(8,128)(2,1)S(1)}, u32[]{:S(2)}, u32[]{:S(2)}) %all-to-all-start) | async-done | bytes 131104 | tf_op jit(solution)/shard_map/all_to_all | solution.py:94
  32.6 0.2 fusion.16
  32.8 0.2 fusion.7
  33.0 0.3 convolution_add_fusion.2
  33.3 0.2 fusion.9
  33.6 0.2 convolution_add_fusion
  33.8 0.6 %copy-done.9 = bf16[256,256]{1,0:T(8,128)(2,1)S(1)} copy-done((bf16[256,256]{1,0:T(8,128)(2,1)S(1)}, bf16[256,256]{1,0:T(8,128)(2,1)}, u32[]{:S(2)}) %copy-start.9) | copy-done | bytes 131096
  34.5 0.2 fusion.10
  34.7 0.7 %copy-done.8 = bf16[256,256]{1,0:T(8,128)(2,1)S(1)} copy-done((bf16[256,256]{1,0:T(8,128)(2,1)S(1)}, bf16[256,256]{1,0:T(8,128)(2,1)}, u32[]{:S(2)}) %copy-start.8) | copy-done | bytes 131096
  35.4 0.2 fusion
  35.6 10.5 %all_to_all.15 = bf16[16,16,256]{2,1,0:T(8,128)(2,1)S(1)} all-to-all(bf16[16,16,256]{2,1,0:T(8,128)(2,1)S(1)} %bitcast.34), channel_id=1, replica_groups=mesh['groups'=2,'seq'=16] {'seq'}, dimensions={0} | all-to-all | bytes 262144 | tf_op jit(solution)/shard_map/all_to_all | solution.py:104
  46.3 0.8 %copy-done.10 = bf16[256,256]{1,0:T(8,128)(2,1)S(1)} copy-done((bf16[256,256]{1,0:T(8,128)(2,1)S(1)}, bf16[256,256]{1,0:T(8,128)(2,1)}, u32[]{:S(2)}) %copy-start.10) | copy-done | bytes 131096
  47.1 0.8 %convolution_convert_fusion.1 = bf16[256,256]{1,0:T(8,128)(2,1)} fusion(bf16[256,256]{1,0:T(8,128)(2,1)S(1)} %copy-done.10, f32[256,768]{1,0:T(8,128)S(1)} %multiply_add_fusion, f32[256,256]{0,1:T(8,128)S(1)} %copy.24), kind=kOutput, calls=%fused_computation.6 | convolution fusion | flops 33751040 | bytes 786432 | tf_op jit(solution)/shard_map/dot_general | solution.py:40
  (31 shorter events, 0.8 us)
Async XLA Ops:
  0.0 11.6 %copy-start = (bf16[256,768]{1,0:T(8,128)(2,1)S(1)}, bf16[256,768]{1,0:T(8,128)(2,1)}, u32[]{:S(2)}) copy-start(bf16[256,768]{1,0:T(8,128)(2,1)} %param.17) | copy-start | bytes 1179652
  0.0 2.6 %copy-start.7 = (f32[256,256]{1,0:T(8,128)S(1)}, f32[256,256]{1,0:T(8,128)}, u32[]{:S(2)}) copy-start(f32[256,256]{1,0:T(8,128)} %param.19) | copy-start | bytes 786436
  1.1 0.7 %copy-start.13 = (f32[256]{0:T(256)S(1)}, f32[256]{0:T(256)}, u32[]{:S(2)}) copy-start(f32[256]{0:T(256)} %param.21) | copy-start | bytes 3076
  4.0 7.5 %copy-start.6 = (bf16[256,256]{1,0:T(8,128)(2,1)S(1)}, bf16[256,256]{1,0:T(8,128)(2,1)}, u32[]{:S(2)}) copy-start(bf16[256,256]{1,0:T(8,128)(2,1)} %param.15) | copy-start | bytes 393220
  4.0 15.5 %all-to-all-start.1 = ((bf16[16,16,256]{2,1,0:T(8,128)(2,1)}), bf16[16,16,256]{2,1,0:T(8,128)(2,1)S(1)}, u32[]{:S(2)}, u32[]{:S(2)}) async-start(bf16[16,16,256]{2,1,0:T(8,128)(2,1)} %bitcast.5), calls=%async_computation.1 | async-start | bytes 262144 | tf_op jit(solution)/shard_map/all_to_all | solution.py:94
  11.6 0.7 %copy-start.12 = (f32[256]{0:T(256)S(1)}, f32[256]{0:T(256)}, u32[]{:S(2)}) copy-start(f32[256]{0:T(256)} %param.16) | copy-start | bytes 3076
  12.3 2.7 %copy-start.11 = (f32[3,768]{1,0:T(4,128)S(1)}, f32[3,768]{1,0:T(4,128)}, u32[]{:S(2)}) copy-start(f32[3,768]{1,0:T(4,128)} %param.18) | copy-start | bytes 27652
  12.6 3.1 %collective-permute-start = (bf16[2,768]{1,0:T(2,128)(2,1)S(1)}, bf16[2,768]{1,0:T(2,128)(2,1)S(1)}, u32[]{:S(2)}, u32[]{:S(2)}) collective-permute-start(bf16[2,768]{1,0:T(2,128)(2,1)S(1)} %slice.103), channel_id=1, source_target_pairs={{0,1},{1,2},{2,3},{3,4},{4,5},{5,6},{6,7},{7,8},{8,9},{9,10},{10,1... | collective-permute-start | bytes 9224 | tf_op jit(solution)/shard_map/ppermute | solution.py:66
  16.1 8.6 %copy-start.5 = (bf16[512,256]{1,0:T(8,128)(2,1)S(1)}, bf16[512,256]{1,0:T(8,128)(2,1)}, u32[]{:S(2)}) copy-start(bf16[512,256]{1,0:T(8,128)(2,1)} %constant.51.clone) | copy-start | bytes 786436
  19.4 13.1 %all-to-all-start = ((bf16[16,16,256]{2,1,0:T(8,128)(2,1)}), bf16[16,16,256]{2,1,0:T(8,128)(2,1)S(1)}, u32[]{:S(2)}, u32[]{:S(2)}) async-start(bf16[16,16,256]{2,1,0:T(8,128)(2,1)} %bitcast.1), calls=%async_computation | async-start | bytes 262144 | tf_op jit(solution)/shard_map/all_to_all | solution.py:94
  24.6 1.0 %copy-start.1 = (f32[256,256]{1,0:T(8,128)S(1)}, f32[256,256]{1,0:T(8,128)}, u32[]{:S(2)}) copy-start(f32[256,256]{1,0:T(8,128)} %constant.55.clone) | copy-start | bytes 786436
  24.7 1.0 %copy-start.2 = (f32[256,256]{1,0:T(8,128)S(1)}, f32[256,256]{1,0:T(8,128)}, u32[]{:S(2)}) copy-start(f32[256,256]{1,0:T(8,128)} %constant.54.clone) | copy-start | bytes 786436
  24.7 1.1 %copy-start.3 = (bf16[256,512]{1,0:T(8,128)(2,1)S(1)}, bf16[256,512]{1,0:T(8,128)(2,1)}, u32[]{:S(2)}) copy-start(bf16[256,512]{1,0:T(8,128)(2,1)} %constant.58) | copy-start | bytes 786436
  25.8 0.9 %copy-start.4 = (bf16[256,512]{1,0:T(8,128)(2,1)S(1)}, bf16[256,512]{1,0:T(8,128)(2,1)}, u32[]{:S(2)}) copy-start(bf16[256,512]{1,0:T(8,128)(2,1)} %constant.59) | copy-start | bytes 786436
  33.6 0.9 %copy-start.9 = (bf16[256,256]{1,0:T(8,128)(2,1)S(1)}, bf16[256,256]{1,0:T(8,128)(2,1)}, u32[]{:S(2)}) copy-start(bf16[256,256]{1,0:T(8,128)(2,1)} %constant.60) | copy-start | bytes 393220
  34.5 0.9 %copy-start.8 = (bf16[256,256]{1,0:T(8,128)(2,1)S(1)}, bf16[256,256]{1,0:T(8,128)(2,1)}, u32[]{:S(2)}) copy-start(bf16[256,256]{1,0:T(8,128)(2,1)} %constant.61) | copy-start | bytes 393220
  46.1 0.9 %copy-start.10 = (bf16[256,256]{1,0:T(8,128)(2,1)S(1)}, bf16[256,256]{1,0:T(8,128)(2,1)}, u32[]{:S(2)}) copy-start(bf16[256,256]{1,0:T(8,128)(2,1)} %param.22) | copy-start | bytes 393220

commit v2 on v1

--- a/solution.py
+++ b/solution.py
@@ -1,9 +1,12 @@
+import functools
 import math
 
 import jax
 import jax.numpy as jnp
 import numpy as np
 from jax import lax
+from jax.experimental import pallas as pl
+from jax.experimental.pallas import tpu as pltpu
 from jax.sharding import PartitionSpec as P
 
 epsilon = 1e-06
@@ -104,8 +107,235 @@
     return lax.all_to_all(split, "seq", 0, 0, tiled=True).reshape(mixed.shape)
 
 
+def far_first(devices):
+    return sorted(range(1, devices), key=lambda off: (abs(off - devices // 2), off))
+
+
+def rms_normed(rows, gain):
+    rows = rows.astype(f32)
+    mean_sq = jnp.mean(rows * rows, axis=-1, keepdims=True)
+    return (rows * lax.rsqrt(mean_sq + epsilon) * gain).astype(bf16)
+
+
+def kernel(
+    devices,
+    tokens_hbm,
+    gain_ref,
+    w_in_hbm,
+    short_ref,
+    long_hbm,
+    med_hbm,
+    skip_ref,
+    w_out_hbm,
+    first_hbm,
+    middle_hbm,
+    last_hbm,
+    tw_cos_hbm,
+    tw_sin_hbm,
+    out_ref,
+    tokens,
+    w_in,
+    long_taps,
+    med,
+    w_out,
+    first,
+    middle,
+    last,
+    tw_cos,
+    tw_sin,
+    halo,
+    extended,
+    sends,
+    arrivals,
+    local_sem,
+    halo_sem,
+    send_sem,
+    recv_sem,
+):
+    me = lax.axis_index("seq")
+    rows, width = tokens.shape
+    offsets = far_first(devices)
+    rim = halo.shape[0]
+    loads = [
+        pltpu.make_async_copy(source, target, local_sem.at[num])
+        for num, (source, target) in enumerate(
+            [
+                (long_hbm, long_taps),
+                (med_hbm, med),
+                (tokens_hbm, tokens),
+                (w_in_hbm, w_in),
+                (first_hbm, first),
+                (tw_cos_hbm, tw_cos),
+                (tw_sin_hbm, tw_sin),
+                (middle_hbm, middle),
+                (last_hbm, last),
+                (w_out_hbm, w_out),
+            ]
+        )
+    ]
+    for load in loads:
+        load.start()
+    barrier = pltpu.get_barrier_semaphore()
+    for off in offsets:
+        pl.semaphore_signal(
+            barrier,
+            inc=1,
+            device_id={"seq": lax.rem(me + off, devices)},
+            device_id_type=pl.DeviceIdType.MESH,
+        )
+
+    def exchange(phase):
+        copies = []
+        for off in offsets:
+            peer = lax.rem(me + off, devices)
+            copy = pltpu.make_async_remote_copy(
+                src_ref=sends.at[phase, peer],
+                dst_ref=arrivals.at[phase, me],
+                send_sem=send_sem.at[phase, off],
+                recv_sem=recv_sem.at[phase, off],
+                device_id={"seq": peer},
+                device_id_type=pl.DeviceIdType.MESH,
+            )
+            copy.start()
+            copies.append(copy)
+        arrivals[phase, me] = sends[phase, me]
+        return copies
+
+    def arrived(phase, copies):
+        for copy in copies:
+            copy.wait_recv()
+        return arrivals[phase].reshape(width, rows)
+
+    loads[0].wait()
+    loads[1].wait()
+
+    @pl.when(me == 0)
+    def _():
+        long_taps[0 : med.shape[0], :] += med[...]
+        long_taps[0:1, :] += skip_ref[...]
+
+    sends[0] = long_taps[...].T.astype(bf16).reshape(sends.shape[1:])
+    loads[2].wait()
+    pl.semaphore_wait(barrier, devices - 1)
+    halo_copy = pltpu.make_async_remote_copy(
+        src_ref=tokens.at[pl.ds(rows - rim, rim)],
+        dst_ref=halo,
+        send_sem=halo_sem.at[0],
+        recv_sem=halo_sem.at[1],
+        device_id={"seq": lax.rem(me + 1, devices)},
+        device_id_type=pl.DeviceIdType.MESH,
+    )
+
+    @pl.when(me < devices - 1)
+    def _():
+        halo_copy.start()
+
+    filter_copies = exchange(0)
+    normed = rms_normed(tokens[...], gain_ref[...])
+    loads[3].wait()
+    extended[rim:, width:] = dot(normed, w_in[:, width:]).astype(bf16).astype(f32)
+
+    @pl.when(me == 0)
+    def _():
+        extended[0:rim, :] = jnp.zeros((rim, 3 * width), f32)
+
+    @pl.when(me > 0)
+    def _():
+        halo_copy.wait_recv()
+        extended[0:rim, :] = dot(rms_normed(halo[...], gain_ref[...]), w_in[...]).astype(bf16).astype(f32)
+
+    def mix(part):
+        lanes = pl.ds(part * width, width)
+        total = short_ref[0:1, lanes] * extended[rim : rim + rows, lanes]
+        for tap in range(1, short_ref.shape[0]):
+            total = total + short_ref[tap : tap + 1, lanes] * extended[rim - tap : rim - tap + rows, lanes]
+        return total
+
+    sends[1] = (mix(1) * mix(2)).T.astype(bf16).reshape(sends.shape[1:])
+    signal_copies = exchange(1)
+
+    extended[rim:, :width] = dot(normed, w_in[:, :width]).astype(bf16).astype(f32)
+    query = mix(0).T
+    for load in loads[4:]:
+        load.wait()
+
+    def spectrum(block):
+        part = dot(first[...], block)
+        re, im = part[:width], part[width:]
+        turned_re = (re * tw_cos[...] + im * tw_sin[...]).astype(bf16)
+        turned_im = (im * tw_cos[...] - re * tw_sin[...]).astype(bf16)
+        spec = dot(turned_re, middle[:rows]) + dot(turned_im, middle[rows:])
+        return spec[:, :rows], spec[:, rows:]
+
+    gr, gi = spectrum(arrived(0, filter_copies))
+    sr, si = spectrum(arrived(1, signal_copies))
+    back = dot((sr * gi + si * gr).astype(bf16), middle[:rows]) + dot(
+        (sr * gr - si * gi).astype(bf16), middle[rows:]
+    )
+    im, re = back[:, :rows], back[:, rows:]
+    mixed = dot(last[:, :width], (re * tw_cos[...] - im * tw_sin[...]).astype(bf16)) + dot(
+        last[:, width:], (re * tw_sin[...] + im * tw_cos[...]).astype(bf16)
+    )
+    sends[2] = mixed.astype(bf16).reshape(sends.shape[1:])
+    result_copies = exchange(2)
+    gated = (query * arrived(2, result_copies).astype(f32)).T.astype(bf16)
+    out_ref[...] = dot(gated, w_out[...]).astype(bf16)
+
+    @pl.when(me < devices - 1)
+    def _():
+        halo_copy.wait_send()
+
+    for copy in filter_copies + signal_copies + result_copies:
+        copy.wait_send()
+
+
+def fused(tokens, norm_gain, w_in, short_filter, long_filter, medium_filter, skip_gain, w_out):
+    rows, width = tokens.shape
+    devices = lax.axis_size("seq")
+    chans = width // devices
+    consts = [jnp.asarray(t) for t in tables(devices, rows, chans)]
+    rim = 16
+    whole = pl.BlockSpec(memory_space=pltpu.VMEM)
+    far = pl.BlockSpec(memory_space=pl.ANY)
+    held = [tokens, w_in, long_filter, medium_filter, w_out] + consts
+    return pl.pallas_call(
+        functools.partial(kernel, devices),
+        out_shape=jax.ShapeDtypeStruct((rows, width), bf16),
+        in_specs=[far, whole, far, whole, far, far, whole, far] + [far] * len(consts),
+        out_specs=whole,
+        scratch_shapes=[pltpu.VMEM(a.shape, a.dtype) for a in held]
+        + [
+            pltpu.VMEM((rim, width), bf16),
+            pltpu.VMEM((rim + rows, 3 * width), f32),
+            pltpu.VMEM((3, devices, chans, rows), bf16),
+            pltpu.VMEM((3, devices, chans, rows), bf16),
+            pltpu.SemaphoreType.DMA((len(held),)),
+            pltpu.SemaphoreType.DMA((2,)),
+            pltpu.SemaphoreType.DMA((3, devices)),
+            pltpu.SemaphoreType.DMA((3, devices)),
+        ],
+        compiler_params=pltpu.CompilerParams(collective_id=0, has_side_effects=True),
+    )(
+        tokens,
+        norm_gain.reshape(1, width),
+        w_in,
+        short_filter,
+        long_filter,
+        medium_filter,
+        skip_gain.reshape(1, width),
+        w_out,
+        *consts,
+    )
+
+
 def solution(mesh):
     placed = (P(("groups", "seq"), None), P(), P(), P(), P("seq", None), P(), P(), P())
+
+    def step(tokens, norm_gain, w_in, short_filter, long_filter, medium_filter, skip_gain, w_out):
+        chans = tokens.shape[1] // mesh.shape["seq"]
+        body = fused if chans % 16 == 0 else local
+        return body(tokens, norm_gain, w_in, short_filter, long_filter, medium_filter, skip_gain, w_out)
+
     return jax.shard_map(
-        local, mesh=mesh, in_specs=placed, out_specs=P(("groups", "seq"), None), check_vma=False
-    )
+        step, mesh=mesh, in_specs=placed, out_specs=P(("groups", "seq"), None), check_vma=False
+    )

time: 48.4 us -> 24.6 us (0.51)
  Pallas kernels: 0 us -> 22.9 us
  starting transfers between devices: 15 us -> 0 us
  blocking collectives: 10.5 us -> 0 us
  waiting for transfers between devices: 8.96 us -> 0 us
  local copies, waits for them, and re-layouts: 7.76 us -> 1.57 us
  matrix products: 3.49 us -> 0 us
  other arithmetic: 1.83 us -> 0 us
    pallas_call x0 -> x1, Pallas kernels: none -> 22.9 us  [fused(): pl.pallas_call(functools.partial(kernel, devices), out_shape=jax.ShapeDty...]
    all_to_all x2 -> x0, starting transfers between devices: 12.7 us -> none  [spread(): lax.all_to_all(split, 'seq', 0, 0, tiled=True).reshape(chan_width, tok_rows)]
    all_to_all x1 -> x0, blocking collectives: 10.5 us -> none  [spread_back(): return lax.all_to_all(split, 'seq', 0, 0, tiled=True).reshape(mixed.shape)]
    all_to_all x2 -> x0, waiting for transfers between devices: 8.2 us -> none  [spread(): lax.all_to_all(split, 'seq', 0, 0, tiled=True).reshape(chan_width, tok_rows)]
    unnamed x30 -> x1, local copies, waits for them, and re-layouts: 6.2 us -> 1.57 us
    dot_general x12 -> x0, matrix products: 3.49 us -> none  [dot(): return jnp.dot(a, b, preferred_element_type=f32)]
    ppermute x1 -> x0, starting transfers between devices: 2.31 us -> none  [from_behind(): return lax.ppermute(array, axis, pairs)]
    add x2 -> x0, other arithmetic: 0.96 us -> none  [the longest x1 0.7 us: local(): med = med.at[0].add(skip_gain)]
  transfers between devices with their start and end apart: 3 -> 0, of which waited for: 3 -> 0; matrix products, arithmetic and copies ran while one was open for 5% -> 0% of each run, Pallas kernels for 0% -> 0%
where the time goes in v2:
time: 24.6 us; the launch traced here: 24.4 us
  Pallas kernels  22.9 us (93%)
  local copies, waits for them, and re-layouts  1.57 us (6%)
    pallas_call x1, Pallas kernels, fused(): pl.pallas_call(functools.partial(kernel, devices), out_shape=jax.ShapeDty...  22.9 us
    unnamed x1, local copies, waits for them, and re-layouts  1.57 us

profile of v2, /device:TPU:0, one launch (start us, length us, event | category | flops | bytes accessed | tf_op | source)
XLA Modules:
  0.0 24.4 jit_solution(16759944734156595345)
XLA Ops:
  0.0 22.9 %shard_map.127 = bf16[256,256]{1,0:T(8,128)(2,1)} custom-call(bf16[256,256]{1,0:T(8,128)(2,1)} %tokens_hbm.1, f32[1,256]{1,0:T(1,128)} %bitcast.2, bf16[256,768]{1,0:T(8,128)(2,1)} %w_in_hbm.1, f32[3,768]{1,0:T(4,128)} %short_ref.1, f32[256,256]{1,0:T(8,128)} %long_hbm.1, f32[128,256]{1,0:T(8,128)} %med_hbm.1, f32[1,256]{1,0:T(1,128)} %bitcast.3, ...), custom_call_target="tpu_custom_call" | custom-call | tf_op jit(solution)/shard_map/pallas_call | solution.py:301
  22.9 1.6 %copy.15 = bf16[256,256]{1,0:T(8,128)(2,1)} copy(bf16[256,256]{1,0:T(8,128)(2,1)} %shard_map.127) | data formatting | bytes 262144

commit v3 on v2

--- a/solution.py
+++ b/solution.py
@@ -107,10 +107,6 @@
     return lax.all_to_all(split, "seq", 0, 0, tiled=True).reshape(mixed.shape)
 
 
-def far_first(devices):
-    return sorted(range(1, devices), key=lambda off: (abs(off - devices // 2), off))
-
-
 def rms_normed(rows, gain):
     rows = rows.astype(f32)
     mean_sq = jnp.mean(rows * rows, axis=-1, keepdims=True)
@@ -120,12 +116,12 @@
 def kernel(
     devices,
     tokens_hbm,
-    gain_ref,
+    gain_hbm,
     w_in_hbm,
-    short_ref,
+    short_hbm,
     long_hbm,
     med_hbm,
-    skip_ref,
+    skip_hbm,
     w_out_hbm,
     first_hbm,
     middle_hbm,
@@ -134,9 +130,12 @@
     tw_sin_hbm,
     out_ref,
     tokens,
+    gain_ref,
     w_in,
+    short_ref,
     long_taps,
     med,
+    skip_ref,
     w_out,
     first,
     middle,
@@ -145,6 +144,7 @@
     tw_sin,
     halo,
     extended,
+    signal,
     sends,
     arrivals,
     local_sem,
@@ -154,16 +154,27 @@
 ):
     me = lax.axis_index("seq")
     rows, width = tokens.shape
-    offsets = far_first(devices)
+    offsets = range(1, devices)
     rim = halo.shape[0]
+    barrier = pltpu.get_barrier_semaphore()
+    for off in offsets:
+        pl.semaphore_signal(
+            barrier,
+            inc=1,
+            device_id={"seq": lax.rem(me + off, devices)},
+            device_id_type=pl.DeviceIdType.MESH,
+        )
     loads = [
         pltpu.make_async_copy(source, target, local_sem.at[num])
         for num, (source, target) in enumerate(
             [
+                (tokens_hbm, tokens),
+                (gain_hbm, gain_ref),
+                (w_in_hbm, w_in),
+                (short_hbm, short_ref),
                 (long_hbm, long_taps),
                 (med_hbm, med),
-                (tokens_hbm, tokens),
-                (w_in_hbm, w_in),
+                (skip_hbm, skip_ref),
                 (first_hbm, first),
                 (tw_cos_hbm, tw_cos),
                 (tw_sin_hbm, tw_sin),
@@ -175,14 +186,6 @@
     ]
     for load in loads:
         load.start()
-    barrier = pltpu.get_barrier_semaphore()
-    for off in offsets:
-        pl.semaphore_signal(
-            barrier,
-            inc=1,
-            device_id={"seq": lax.rem(me + off, devices)},
-            device_id_type=pl.DeviceIdType.MESH,
-        )
 
     def exchange(phase):
         copies = []
@@ -206,8 +209,28 @@
             copy.wait_recv()
         return arrivals[phase].reshape(width, rows)
 
-    loads[0].wait()
-    loads[1].wait()
+    def project(part_normed, begin):
+        return dot(part_normed, w_in[:, begin:]).astype(bf16).astype(f32)
+
+    def mix(part, begin, count):
+        lanes = pl.ds(part * width, width)
+        total = short_ref[0:1, lanes] * extended[rim + begin : rim + begin + count, lanes]
+        for tap in range(1, short_ref.shape[0]):
+            start = rim + begin - tap
+            total = total + short_ref[tap : tap + 1, lanes] * extended[start : start + count, lanes]
+        return total
+
+    def turn_signal(begin, count):
+        block = signal[begin : begin + count, :].T.astype(bf16)
+        sends[1, :, :, begin : begin + count] = block.reshape(devices, width // devices, count)
+
+    for load in loads[:3]:
+        load.wait()
+    normed = rms_normed(tokens[...], gain_ref[...])
+    extended[rim:, width:] = project(normed, width)
+    extended[0:rim, :] = jnp.zeros((rim, 3 * width), f32)
+    for load in loads[3:7]:
+        load.wait()
 
     @pl.when(me == 0)
     def _():
@@ -215,7 +238,8 @@
         long_taps[0:1, :] += skip_ref[...]
 
     sends[0] = long_taps[...].T.astype(bf16).reshape(sends.shape[1:])
-    loads[2].wait()
+    signal[...] = mix(1, 0, rows) * mix(2, 0, rows)
+    turn_signal(rows // 2, rows // 2)
     pl.semaphore_wait(barrier, devices - 1)
     halo_copy = pltpu.make_async_remote_copy(
         src_ref=tokens.at[pl.ds(rows - rim, rim)],
@@ -231,32 +255,19 @@
         halo_copy.start()
 
     filter_copies = exchange(0)
-    normed = rms_normed(tokens[...], gain_ref[...])
-    loads[3].wait()
-    extended[rim:, width:] = dot(normed, w_in[:, width:]).astype(bf16).astype(f32)
-
-    @pl.when(me == 0)
-    def _():
-        extended[0:rim, :] = jnp.zeros((rim, 3 * width), f32)
 
     @pl.when(me > 0)
     def _():
         halo_copy.wait_recv()
-        extended[0:rim, :] = dot(rms_normed(halo[...], gain_ref[...]), w_in[...]).astype(bf16).astype(f32)
-
-    def mix(part):
-        lanes = pl.ds(part * width, width)
-        total = short_ref[0:1, lanes] * extended[rim : rim + rows, lanes]
-        for tap in range(1, short_ref.shape[0]):
-            total = total + short_ref[tap : tap + 1, lanes] * extended[rim - tap : rim - tap + rows, lanes]
-        return total
-
-    sends[1] = (mix(1) * mix(2)).T.astype(bf16).reshape(sends.shape[1:])
+        extended[0:rim, :] = project(rms_normed(halo[...], gain_ref[...]), 0)
+        signal[0:rim, :] = mix(1, 0, rim) * mix(2, 0, rim)
+
+    turn_signal(0, rows // 2)
     signal_copies = exchange(1)
 
     extended[rim:, :width] = dot(normed, w_in[:, :width]).astype(bf16).astype(f32)
-    query = mix(0).T
-    for load in loads[4:]:
+    query = mix(0, 0, rows).T
+    for load in loads[7:]:
         load.wait()
 
     def spectrum(block):
@@ -295,27 +306,7 @@
     chans = width // devices
     consts = [jnp.asarray(t) for t in tables(devices, rows, chans)]
     rim = 16
-    whole = pl.BlockSpec(memory_space=pltpu.VMEM)
-    far = pl.BlockSpec(memory_space=pl.ANY)
-    held = [tokens, w_in, long_filter, medium_filter, w_out] + consts
-    return pl.pallas_call(
-        functools.partial(kernel, devices),
-        out_shape=jax.ShapeDtypeStruct((rows, width), bf16),
-        in_specs=[far, whole, far, whole, far, far, whole, far] + [far] * len(consts),
-        out_specs=whole,
-        scratch_shapes=[pltpu.VMEM(a.shape, a.dtype) for a in held]
-        + [
-            pltpu.VMEM((rim, width), bf16),
-            pltpu.VMEM((rim + rows, 3 * width), f32),
-            pltpu.VMEM((3, devices, chans, rows), bf16),
-            pltpu.VMEM((3, devices, chans, rows), bf16),
-            pltpu.SemaphoreType.DMA((len(held),)),
-            pltpu.SemaphoreType.DMA((2,)),
-            pltpu.SemaphoreType.DMA((3, devices)),
-            pltpu.SemaphoreType.DMA((3, devices)),
-        ],
-        compiler_params=pltpu.CompilerParams(collective_id=0, has_side_effects=True),
-    )(
+    held = [
         tokens,
         norm_gain.reshape(1, width),
         w_in,
@@ -325,7 +316,26 @@
         skip_gain.reshape(1, width),
         w_out,
         *consts,
-    )
+    ]
+    return pl.pallas_call(
+        functools.partial(kernel, devices),
+        out_shape=pltpu.VMEM((rows, width), bf16),
+        in_specs=[pl.BlockSpec(memory_space=pl.ANY)] * len(held),
+        out_specs=pl.BlockSpec(memory_space=pltpu.VMEM),
+        scratch_shapes=[pltpu.VMEM(a.shape, a.dtype) for a in held]
+        + [
+            pltpu.VMEM((rim, width), bf16),
+            pltpu.VMEM((rim + rows, 3 * width), f32),
+            pltpu.VMEM((rows, width), f32),
+            pltpu.VMEM((3, devices, chans, rows), bf16),
+            pltpu.VMEM((3, devices, chans, rows), bf16),
+            pltpu.SemaphoreType.DMA((len(held),)),
+            pltpu.SemaphoreType.DMA((2,)),
+            pltpu.SemaphoreType.DMA((3, devices)),
+            pltpu.SemaphoreType.DMA((3, devices)),
+        ],
+        compiler_params=pltpu.CompilerParams(collective_id=0, has_side_effects=True),
+    )(*held)
 
 
 def solution(mesh):

time: 24.6 us -> 21.2 us (0.86)
  Pallas kernels: 22.9 us -> 20.4 us
  local copies, waits for them, and re-layouts: 1.57 us -> 0.66 us
    pallas_call x1, Pallas kernels: 22.9 us -> 20.4 us  [fused(): pl.pallas_call(functools.partial(kernel, devices), out_shape=pltpu.VMEM((...]
    unnamed x1, local copies, waits for them, and re-layouts: 1.57 us -> 0.66 us
where the time goes in v3:
time: 21.2 us; the launch traced here: 21.1 us
  Pallas kernels  20.4 us (96%)
  local copies, waits for them, and re-layouts  0.66 us (3%)
    pallas_call x1, Pallas kernels, fused(): pl.pallas_call(functools.partial(kernel, devices), out_shape=pltpu.VMEM((...  20.4 us
    unnamed x1, local copies, waits for them, and re-layouts  0.66 us

profile of v3, /device:TPU:0, one launch (start us, length us, event | category | flops | bytes accessed | tf_op | source)
XLA Modules:
  0.0 21.1 jit_solution(14399533471190841370)
XLA Ops:
  0.0 20.4 %shard_map.127 = bf16[256,256]{1,0:T(8,128)(2,1)S(1)} custom-call(bf16[256,256]{1,0:T(8,128)(2,1)} %tokens_hbm.1, f32[1,256]{1,0:T(1,128)} %bitcast.2, bf16[256,768]{1,0:T(8,128)(2,1)} %w_in_hbm.1, f32[3,768]{1,0:T(4,128)} %short_hbm.1, f32[256,256]{1,0:T(8,128)} %long_hbm.1, f32[128,256]{1,0:T(8,128)} %med_hbm.1, f32[1,256]{1,0:T(1,128)} %bitcast.3, ...), custom_call_target="tpu_custom_call" | custom-call | tf_op jit(solution)/shard_map/pallas_call | solution.py:320
  20.4 0.7 %copy.15 = bf16[256,256]{1,0:T(8,128)(2,1)} copy(bf16[256,256]{1,0:T(8,128)(2,1)S(1)} %shard_map.127) | data formatting | bytes 262144

commit v4 on v3

--- a/solution.py
+++ b/solution.py
@@ -188,25 +188,28 @@
         load.start()
 
     def exchange(phase):
-        copies = []
         for off in offsets:
             peer = lax.rem(me + off, devices)
-            copy = pltpu.make_async_remote_copy(
+            pltpu.make_async_remote_copy(
                 src_ref=sends.at[phase, peer],
                 dst_ref=arrivals.at[phase, me],
-                send_sem=send_sem.at[phase, off],
-                recv_sem=recv_sem.at[phase, off],
+                send_sem=send_sem.at[phase],
+                recv_sem=recv_sem.at[phase],
                 device_id={"seq": peer},
                 device_id_type=pl.DeviceIdType.MESH,
-            )
-            copy.start()
-            copies.append(copy)
+            ).start()
         arrivals[phase, me] = sends[phase, me]
-        return copies
+        return pltpu.make_async_remote_copy(
+            src_ref=sends.at[phase, pl.ds(0, devices - 1)],
+            dst_ref=arrivals.at[phase, pl.ds(0, devices - 1)],
+            send_sem=send_sem.at[phase],
+            recv_sem=recv_sem.at[phase],
+            device_id={"seq": lax.rem(me + 1, devices)},
+            device_id_type=pl.DeviceIdType.MESH,
+        )
 
     def arrived(phase, copies):
-        for copy in copies:
-            copy.wait_recv()
+        copies.wait_recv()
         return arrivals[phase].reshape(width, rows)
 
     def project(part_normed, begin):
@@ -296,8 +299,8 @@
     def _():
         halo_copy.wait_send()
 
-    for copy in filter_copies + signal_copies + result_copies:
-        copy.wait_send()
+    for copies in (filter_copies, signal_copies, result_copies):
+        copies.wait_send()
 
 
 def fused(tokens, norm_gain, w_in, short_filter, long_filter, medium_filter, skip_gain, w_out):
@@ -331,8 +334,8 @@
             pltpu.VMEM((3, devices, chans, rows), bf16),
             pltpu.SemaphoreType.DMA((len(held),)),
             pltpu.SemaphoreType.DMA((2,)),
-            pltpu.SemaphoreType.DMA((3, devices)),
-            pltpu.SemaphoreType.DMA((3, devices)),
+            pltpu.SemaphoreType.DMA((3,)),
+            pltpu.SemaphoreType.DMA((3,)),
         ],
         compiler_params=pltpu.CompilerParams(collective_id=0, has_side_effects=True),
     )(*held)

time: 21.2 us -> 20.3 us (0.958)
  Pallas kernels: 20.4 us -> 19.5 us
    pallas_call x1, Pallas kernels: 20.4 us -> 19.5 us  [fused(): pl.pallas_call(functools.partial(kernel, devices), out_shape=pltpu.VMEM((...]
where the time goes in v4:
time: 20.3 us; the launch traced here: 20.2 us
  Pallas kernels  19.5 us (96%)
  local copies, waits for them, and re-layouts  0.66 us (3%)
    pallas_call x1, Pallas kernels, fused(): pl.pallas_call(functools.partial(kernel, devices), out_shape=pltpu.VMEM((...  19.5 us
    unnamed x1, local copies, waits for them, and re-layouts  0.66 us

profile of v4, /device:TPU:0, one launch (start us, length us, event | category | flops | bytes accessed | tf_op | source)
XLA Modules:
  0.0 20.2 jit_solution(13262776825217790454)
XLA Ops:
  0.0 19.5 %shard_map.127 = bf16[256,256]{1,0:T(8,128)(2,1)S(1)} custom-call(bf16[256,256]{1,0:T(8,128)(2,1)} %tokens_hbm.1, f32[1,256]{1,0:T(1,128)} %bitcast.2, bf16[256,768]{1,0:T(8,128)(2,1)} %w_in_hbm.1, f32[3,768]{1,0:T(4,128)} %short_hbm.1, f32[256,256]{1,0:T(8,128)} %long_hbm.1, f32[128,256]{1,0:T(8,128)} %med_hbm.1, f32[1,256]{1,0:T(1,128)} %bitcast.3, ...), custom_call_target="tpu_custom_call" | custom-call | tf_op jit(solution)/shard_map/pallas_call | solution.py:323
  19.5 0.7 %copy.15 = bf16[256,256]{1,0:T(8,128)(2,1)} copy(bf16[256,256]{1,0:T(8,128)(2,1)S(1)} %shard_map.127) | data formatting | bytes 262144

commit v5 on v4

--- a/solution.py
+++ b/solution.py
@@ -188,7 +188,7 @@
         load.start()
 
     def exchange(phase):
-        for off in offsets:
+        for off in (offsets if phase else reversed(offsets)):
             peer = lax.rem(me + off, devices)
             pltpu.make_async_remote_copy(
                 src_ref=sends.at[phase, peer],
@@ -276,23 +276,24 @@
     def spectrum(block):
         part = dot(first[...], block)
         re, im = part[:width], part[width:]
-        turned_re = (re * tw_cos[...] + im * tw_sin[...]).astype(bf16)
-        turned_im = (im * tw_cos[...] - re * tw_sin[...]).astype(bf16)
-        spec = dot(turned_re, middle[:rows]) + dot(turned_im, middle[rows:])
+        turned = jnp.concatenate(
+            [re * tw_cos[...] + im * tw_sin[...], im * tw_cos[...] - re * tw_sin[...]], axis=1
+        )
+        spec = dot(turned.astype(bf16), middle[...])
         return spec[:, :rows], spec[:, rows:]
 
     gr, gi = spectrum(arrived(0, filter_copies))
     sr, si = spectrum(arrived(1, signal_copies))
-    back = dot((sr * gi + si * gr).astype(bf16), middle[:rows]) + dot(
-        (sr * gr - si * gi).astype(bf16), middle[rows:]
+    prod = jnp.concatenate([sr * gi + si * gr, sr * gr - si * gi], axis=1)
+    back = dot(prod.astype(bf16), middle[...])
+    im, re = back[:, :rows], back[:, rows:]
+    turned = jnp.concatenate(
+        [re * tw_cos[...] - im * tw_sin[...], re * tw_sin[...] + im * tw_cos[...]], axis=0
     )
-    im, re = back[:, :rows], back[:, rows:]
-    mixed = dot(last[:, :width], (re * tw_cos[...] - im * tw_sin[...]).astype(bf16)) + dot(
-        last[:, width:], (re * tw_sin[...] + im * tw_cos[...]).astype(bf16)
-    )
+    mixed = dot(last[...], turned.astype(bf16))
     sends[2] = mixed.astype(bf16).reshape(sends.shape[1:])
     result_copies = exchange(2)
-    gated = (query * arrived(2, result_copies).astype(f32)).T.astype(bf16)
+    gated = (query * arrived(2, result_copies).astype(f32)).astype(bf16).T
     out_ref[...] = dot(gated, w_out[...]).astype(bf16)
 
     @pl.when(me < devices - 1)

time: 20.3 us -> 20.2 us (level)
  no operation moved by 1% of the time
where the time goes in v5:
time: 20.2 us; the launch traced here: 20.1 us
  Pallas kernels  19.4 us (96%)
  local copies, waits for them, and re-layouts  0.66 us (3%)
    pallas_call x1, Pallas kernels, fused(): pl.pallas_call(functools.partial(kernel, devices), out_shape=pltpu.VMEM((...  19.4 us
    unnamed x1, local copies, waits for them, and re-layouts  0.66 us

profile of v5, /device:TPU:0, one launch (start us, length us, event | category | flops | bytes accessed | tf_op | source)
XLA Modules:
  0.0 20.1 jit_solution(43063110098924804)
XLA Ops:
  0.0 19.4 %shard_map.127 = bf16[256,256]{1,0:T(8,128)(2,1)S(1)} custom-call(bf16[256,256]{1,0:T(8,128)(2,1)} %tokens_hbm.1, f32[1,256]{1,0:T(1,128)} %bitcast.2, bf16[256,768]{1,0:T(8,128)(2,1)} %w_in_hbm.1, f32[3,768]{1,0:T(4,128)} %short_hbm.1, f32[256,256]{1,0:T(8,128)} %long_hbm.1, f32[128,256]{1,0:T(8,128)} %med_hbm.1, f32[1,256]{1,0:T(1,128)} %bitcast.3, ...), custom_call_target="tpu_custom_call" | custom-call | tf_op jit(solution)/shard_map/pallas_call | solution.py:324
  19.4 0.7 %copy.15 = bf16[256,256]{1,0:T(8,128)(2,1)} copy(bf16[256,256]{1,0:T(8,128)(2,1)S(1)} %shard_map.127) | data formatting | bytes 262144
